TPU v7x, 32 devices: a whole 2x2x4 slice. The times are simulated.
32 devices in a mesh: section: 4 (over y, x), seq: 8 (over z, core).
Axes of the slice: x: 2, y: 2, z: 4, core: 2. Of those that a mesh axis runs over, the one named last changes fastest.
Arguments:
- features: bfloat16 [4, 1024, 4096], P('section', 'seq'), may hold values from -6 to 6
- queries: bfloat16 [4, 1024, 4096], P('section', 'seq'), may hold values from -52 to 52
- out_grad: bfloat16 [4, 1024, 4096], P('section', 'seq'), may hold values from -0.375 to 0.375
- doc_ids: int32 [4, 1024], P('section', 'seq'), may hold values from 0 to 3, never falling along the last dimension, each value on 1 to 512 neighbouring positions
- key_weight: bfloat16 [4096, 512], P('section'), may hold values from -0.09375 to 0.09375
Outputs:
- value_weight_grad: float32 [4096, 512], P('seq', 'section')
All inputs are finite; a program needn't handle non-finite values.
Results may differ from a plain program's by a relative error of at most 0.012.
Values may be sent and summed in bfloat16 or wider, within the bound.
A program may use at most 64 MiB of HBM per device.

v0:
```python
import math

import jax
import jax.numpy as jnp
from jax import lax
from jax.sharding import PartitionSpec as P

HQ = 32
KVH = 4
HD = 128
REACH = 4


def prefix_2(part, axis, combine, identity):
    place = lax.axis_index(axis)
    gathered = jax.tree.map(lambda a: lax.all_gather(a, axis), part)
    state = jax.tree.map(lambda a, e: jnp.zeros_like(a) + jnp.asarray(e, a.dtype), part, identity)

    def one(step, state):
        return combine(
            state, jax.tree.map(lambda a: lax.dynamic_index_in_dim(a, step, 0, False), gathered)
        )

    return lax.fori_loop(0, place, one, state)


def shifted(x, axis, by):
    peers = lax.axis_size(axis)
    pairs = [(i, i + by) for i in range(peers) if 0 <= i + by < peers]
    return lax.ppermute(x, axis, pairs)


def join_bounds(earlier, later):
    early_first, early_last, early_start = earlier
    late_first, late_last, late_start = later
    first_id = jnp.where(early_first < 0, late_first, early_first)
    carried = (late_first == late_last) & (early_last == late_last)
    start_pos = jnp.where(late_last < 0, early_start, jnp.where(carried, early_start, late_start))
    last_id = jnp.where(late_last < 0, early_last, late_last)
    return (first_id, last_id, start_pos)


def on_device(features, queries, out_grad, doc_ids, key_weight):
    tokens = features[0]
    tok_count = tokens.shape[0]
    group_size = HQ // KVH
    query_rows = queries[0].reshape(tok_count, KVH, group_size, HD)
    grad_rows = out_grad[0].reshape(tok_count, KVH, group_size, HD)
    doc_local = doc_ids[0]
    full_weight = lax.all_gather(key_weight, "section", axis=0, tiled=True)
    key_sum = jnp.dot(tokens, full_weight, preferred_element_type=jnp.float32)
    keys_local = key_sum.astype(jnp.bfloat16)
    offset = lax.axis_index("seq") * tok_count
    smaller = (doc_local[None, :] < doc_local[:, None]).astype(jnp.int32)
    local_first = offset + jnp.sum(smaller, axis=1)
    summary = (doc_local[0], doc_local[-1], local_first[-1])
    missing = jnp.int32(-1)
    prefix = prefix_2(summary, "seq", join_bounds, (missing, missing, jnp.int32(0)))
    continued = (doc_local == doc_local[0]) & (prefix[1] == doc_local[0])
    doc_start = jnp.where(continued, prefix[2], local_first)
    key_blocks = [keys_local]
    for hop_count in range(1, REACH + 1):
        key_blocks.insert(0, shifted(keys_local, "seq", hop_count))
    window = jnp.concatenate(key_blocks, axis=0)
    window_len = window.shape[0]
    key_pos = offset - REACH * tok_count + jnp.arange(window_len, dtype=jnp.int32)
    query_pos = offset + jnp.arange(tok_count, dtype=jnp.int32)
    visible = (key_pos[None, :] >= doc_start[:, None]) & (key_pos[None, :] <= query_pos[:, None])
    mask_full = visible[:, None, :]
    score_scale = 1.0 / math.sqrt(HD)
    window_heads = window.reshape(window_len, KVH, HD)
    grad_parts = []
    for head_index in range(KVH):
        scores = (
            jnp.einsum(
                "trd,wd->trw",
                query_rows[:, head_index],
                window_heads[:, head_index],
                preferred_element_type=jnp.float32,
            )
            * score_scale
        )
        masked = jnp.where(mask_full, scores, -1e30)
        row_top = jnp.max(masked, axis=2, keepdims=True)
        weights_exp = jnp.where(mask_full, jnp.exp(masked - row_top), 0.0)
        prob_rows = (weights_exp / jnp.sum(weights_exp, axis=2, keepdims=True)).astype(jnp.bfloat16)
        grad_parts.append(
            jnp.einsum(
                "trw,trd->wd",
                prob_rows,
                grad_rows[:, head_index],
                preferred_element_type=jnp.float32,
            )
        )
    window_grad = jnp.concatenate(grad_parts, axis=1)
    slots = [
        window_grad[index_slot * tok_count : (index_slot + 1) * tok_count]
        for index_slot in range(REACH + 1)
    ]
    own_grad = slots[REACH]
    for hop_count in range(1, REACH + 1):
        own_grad = own_grad + shifted(slots[REACH - hop_count], "seq", -hop_count)
    value_grad = own_grad.astype(jnp.bfloat16)
    columns = lax.all_to_all(tokens, "seq", split_axis=1, concat_axis=0, tiled=True)
    grad_block = jnp.einsum(
        "td,tk->dk",
        columns,
        lax.all_gather(value_grad, "seq", axis=0, tiled=True),
        preferred_element_type=jnp.float32,
    )
    return lax.psum_scatter(grad_block, "section", scatter_dimension=1, tiled=True)


def solution(mesh):
    return jax.shard_map(
        on_device,
        mesh=mesh,
        in_specs=(
            P("section", "seq", None),
            P("section", "seq", None),
            P("section", "seq", None),
            P("section", "seq"),
            P("section", None),
        ),
        out_specs=P("seq", "section"),
        check_vma=False,
    )
```

profile of v0, /device:TPU:0, one launch (start us, length us, event | category | flops | bytes accessed | tf_op | source)
XLA Modules:
  0.0 218.9 jit_solution(15497004019534483116)
XLA Ops:
  8.6 1.3 fusion.55
  13.0 1.3 bitcast_dynamic-update-slice_fusion.1
  14.3 10.6 %all-reduce.3 = (s32[8]{0:T(128)S(1)}, s32[8]{0:T(128)S(1)}, s32[8]{0:T(128)S(1)}) all-reduce(s32[8]{0:T(128)S(1)} %bitcast_dynamic-update-slice_fusion.1, s32[8]{0:T(128)S(1)} %bitcast_dynamic-update-slice_fusion, s32[8]{0:T(128)S(1)} %slice_dynamic-update-slice_fusion), channel_id=2, replica_groups=mesh['section'=4,'seq'=8] {'seq'}, use_global_device_ids=true, to_apply=%add | all-reduce | flops 24 | bytes 192 | tf_op jit(solution)/shard_map/all_gather | solution.py:16
  26.7 38.0 %all-gather.5.cloned.1.call-done = bf16[4096,512]{1,0:T(8,128)(2,1)} async-done(((bf16[1024,512]{1,0:T(8,128)(2,1)}), bf16[4096,512]{1,0:T(8,128)(2,1)}) %all-gather.5.cloned.1.call-update) | async-done | bytes 4194320 | tf_op jit(solution)/shard_map/all_gather | solution.py:50
  64.7 3.2 %convolution_convert_fusion = bf16[128,512]{1,0:T(8,128)(2,1)S(1)} fusion(bf16[4096,512]{1,0:T(8,128)(2,1)} %all-gather.5.cloned.1.call-done, bf16[1,128,4096]{2,1,0:T(8,128)(2,1)} %param.7), kind=kOutput, calls=%fused_computation.42 | convolution fusion | flops 536936448 | bytes 5373952 | tf_op jit(solution)/shard_map/dot_general | solution.py:51
  67.9 4.3 %collective-permute-start = (bf16[128,512]{1,0:T(8,128)(2,1)S(1)}, bf16[128,512]{1,0:T(8,128)(2,1)S(1)}, u32[]{:S(2)}, u32[]{:S(2)}) collective-permute-start(bf16[128,512]{1,0:T(8,128)(2,1)S(1)} %convolution_convert_fusion), channel_id=1, source_target_pairs={{0,4},{1,5},{2,6},{3,7},{8,12},{9,13},{10,14},{11,15},{16,20},{17,... | collective-permute-start | bytes 393224 | tf_op jit(solution)/shard_map/ppermute | solution.py:30
  72.3 2.5 %collective-permute-start.1 = (bf16[128,512]{1,0:T(8,128)(2,1)S(1)}, bf16[128,512]{1,0:T(8,128)(2,1)S(1)}, u32[]{:S(2)}, u32[]{:S(2)}) collective-permute-start(bf16[128,512]{1,0:T(8,128)(2,1)S(1)} %convolution_convert_fusion), channel_id=1, source_target_pairs={{0,3},{1,4},{2,5},{3,6},{4,7},{8,11},{9,12},{10,13},{11,14},{12,15... | collective-permute-start | bytes 393224 | tf_op jit(solution)/shard_map/ppermute | solution.py:30
  77.0 2.3 %collective-permute-start.2 = (bf16[128,512]{1,0:T(8,128)(2,1)S(1)}, bf16[128,512]{1,0:T(8,128)(2,1)S(1)}, u32[]{:S(2)}, u32[]{:S(2)}) collective-permute-start(bf16[128,512]{1,0:T(8,128)(2,1)S(1)} %convolution_convert_fusion), channel_id=1, source_target_pairs={{0,2},{1,3},{2,4},{3,5},{4,6},{5,7},{8,10},{9,11},{10,12},{11,13},... | collective-permute-start | bytes 393224 | tf_op jit(solution)/shard_map/ppermute | solution.py:30
  79.2 1.8 collective-permute-start.3
  84.9 1.6 reshape.84
  86.5 1.8 fusion.54
  88.3 3.6 %fusion.59 = (f32[128,8]{0,1:T(8,128)S(1)}, f32[128,8,640]{0,2,1:T(8,128)}) fusion(pred[128,640]{0,1:T(8,128)(4,1)S(1)} %compare_and_fusion, bf16[128,4,8,128]{0,3,2,1:T(8,128)(2,1)S(1)} %bitcast.155, bf16[640,1,128]{2,1,0:T(2,128)(2,1)} %get-tuple-element.87), kind=kOutput, calls=%fused_computation.97 | convolution fusion | flops 171049600 | bytes 3215360 | tf_op jit(solution)/shard_map/sub | solution.py:85
  91.9 2.6 %fusion.58 = (f32[128,8]{0,1:T(8,128)S(1)}, f32[128,8,640]{0,2,1:T(8,128)}) fusion(pred[128,640]{0,1:T(8,128)(4,1)S(1)} %compare_and_fusion, bf16[128,4,8,128]{0,3,2,1:T(8,128)(2,1)S(1)} %bitcast.156, bf16[640,1,128]{2,1,0:T(2,128)(2,1)S(1)} %copy-done.4), kind=kOutput, calls=%fused_computation.96 | convolution fusion | flops 171049600 | bytes 3379200 | tf_op jit(solution)/shard_map/sub | solution.py:85
  94.6 2.6 %fusion.57 = (f32[128,8]{0,1:T(8,128)S(1)}, f32[128,8,640]{0,2,1:T(8,128)}) fusion(pred[128,640]{0,1:T(8,128)(4,1)S(1)} %compare_and_fusion, bf16[128,4,8,128]{0,3,2,1:T(8,128)(2,1)S(1)} %bitcast.157, bf16[640,1,128]{2,1,0:T(2,128)(2,1)S(1)} %get-tuple-element.88), kind=kOutput, calls=%fused_computation.95 | convolution fusion | flops 171049600 | bytes 3379200 | tf_op jit(solution)/shard_map/sub | solution.py:85
  97.2 2.6 %fusion.56 = (f32[128,8]{0,1:T(8,128)S(1)}, f32[128,8,640]{0,2,1:T(8,128)}) fusion(pred[128,640]{0,1:T(8,128)(4,1)S(1)} %compare_and_fusion, bf16[128,4,8,128]{0,3,2,1:T(8,128)(2,1)S(1)} %bitcast.158, bf16[640,1,128]{2,1,0:T(2,128)(2,1)S(1)} %get-tuple-element.90), kind=kOutput, calls=%fused_computation.94 | convolution fusion | flops 171049600 | bytes 3379200 | tf_op jit(solution)/shard_map/sub | solution.py:85
  99.8 2.4 %fusion.27 = f32[640,128]{0,1:T(8,128)S(1)} fusion(f32[128,8,640]{0,2,1:T(8,128)} %get-tuple-element.100, f32[128,8]{0,1:T(8,128)S(1)} %get-tuple-element.99, bf16[128,4,8,128]{0,3,2,1:T(8,128)(2,1)S(1)} %bitcast.151), kind=kOutput, calls=%fused_computation.41 | convolution fusion | flops 169082880 | bytes 3215360 | tf_op jit(solution)/shard_map/trw,trd->wd/dot_general | solution.py:88
  113.9 10.4 %all-to-all-start = ((bf16[128,8,512]{0,2,1:T(8,128)(2,1)}), bf16[128,8,512]{0,2,1:T(8,128)(2,1)S(1)}, u32[]{:S(2)}, u32[]{:S(2)}) async-start(bf16[128,8,512]{0,2,1:T(8,128)(2,1)} %bitcast.35), calls=%async_computation | async-start | bytes 2097152 | tf_op jit(solution)/shard_map/all_to_all | solution.py:104
  124.4 1.4 collective-permute-done.6
  125.8 31.6 %collective-permute-done.7 = f32[128,512]{0,1:T(8,128)S(1)} collective-permute-done((f32[128,512]{0,1:T(8,128)}, f32[128,512]{0,1:T(8,128)S(1)}, u32[]{:S(2)}, u32[]{:S(2)}) %collective-permute-start.7) | collective-permute-done | bytes 262176 | tf_op jit(solution)/shard_map/ppermute | solution.py:30
  158.3 12.3 %all-to-all-done = bf16[128,8,512]{0,2,1:T(8,128)(2,1)S(1)} async-done(((bf16[128,8,512]{0,2,1:T(8,128)(2,1)}), bf16[128,8,512]{0,2,1:T(8,128)(2,1)S(1)}, u32[]{:S(2)}, u32[]{:S(2)}) %all-to-all-start) | async-done | bytes 1048608 | tf_op jit(solution)/shard_map/all_to_all | solution.py:104
  171.1 8.6 %all-gather.7.cloned.1.call-done = bf16[1024,512]{0,1:T(8,128)(2,1)} async-done(((bf16[128,512]{0,1:T(8,128)(2,1)}), bf16[1024,512]{0,1:T(8,128)(2,1)}) %all-gather.7.cloned.1.call-update) | async-done | bytes 1048592 | tf_op jit(solution)/shard_map/all_gather | solution.py:108
  179.7 2.9 %convolution_bitcast_fusion = f32[512,512]{0,1:T(8,128)} fusion(bf16[1024,512]{0,1:T(8,128)(2,1)} %all-gather.7.cloned.1.call-done, bf16[1024,512]{1,0:T(8,128)(2,1)S(1)} %bitcast.159), kind=kOutput, calls=%fused_computation.20 | convolution fusion | flops 536870912 | bytes 3145728 | tf_op jit(solution)/shard_map/td,tk->dk/dot_general | solution.py:105
  182.6 28.0 %reduce-scatter.2.cloned.1.call-done = f32[512,128]{0,1:T(8,128)} async-done(((f32[512,512]{0,1:T(8,128)}), f32[512,128]{0,1:T(8,128)}) %reduce-scatter.2.cloned.1.call-update) | async-done | bytes 262160 | tf_op jit(solution)/shard_map/reduce_scatter | solution.py:111
  210.6 1.8 copy.64
  (60 shorter events, 25.2 us)
Async XLA Ops:
  6.5 58.1 %all-gather.5.cloned.1.call-start = ((), (), s32[]{:S(2)}) async-start(), calls=%async_computation.2 | async-start | bytes 5242880 | tf_op jit(solution)/shard_map/all_gather | solution.py:50
  26.7 48.3 %copy-start.1 = (bf16[1,128,4096]{2,1,0:T(8,128)(2,1)S(1)}, bf16[1,128,4096]{2,1,0:T(8,128)(2,1)}, u32[]{:S(2)}) copy-start(bf16[1,128,4096]{2,1,0:T(8,128)(2,1)} %param.8) | copy-start | bytes 3145732
  26.7 49.6 %copy-start.2 = (bf16[1,128,4096]{2,1,0:T(8,128)(2,1)S(1)}, bf16[1,128,4096]{2,1,0:T(8,128)(2,1)}, u32[]{:S(2)}) copy-start(bf16[1,128,4096]{2,1,0:T(8,128)(2,1)} %param.9) | copy-start | bytes 3145732
  67.9 13.1 %collective-permute-start = (bf16[128,512]{1,0:T(8,128)(2,1)S(1)}, bf16[128,512]{1,0:T(8,128)(2,1)S(1)}, u32[]{:S(2)}, u32[]{:S(2)}) collective-permute-start(bf16[128,512]{1,0:T(8,128)(2,1)S(1)} %convolution_convert_fusion), channel_id=1, source_target_pairs={{0,4},{1,5},{2,6},{3,7},{8,12},{9,13},{10,14},{11,15},{16,20},{17,... | collective-permute-start | bytes 393224 | tf_op jit(solution)/shard_map/ppermute | solution.py:30
  72.3 9.5 %collective-permute-start.1 = (bf16[128,512]{1,0:T(8,128)(2,1)S(1)}, bf16[128,512]{1,0:T(8,128)(2,1)S(1)}, u32[]{:S(2)}, u32[]{:S(2)}) collective-permute-start(bf16[128,512]{1,0:T(8,128)(2,1)S(1)} %convolution_convert_fusion), channel_id=1, source_target_pairs={{0,3},{1,4},{2,5},{3,6},{4,7},{8,11},{9,12},{10,13},{11,14},{12,15... | collective-permute-start | bytes 393224 | tf_op jit(solution)/shard_map/ppermute | solution.py:30
  76.9 11.4 %copy-start.3 = (bf16[1,128,4096]{1,2,0:T(8,128)(2,1)S(1)}, bf16[1,128,4096]{1,2,0:T(8,128)(2,1)}, u32[]{:S(2)}) copy-start(bf16[1,128,4096]{1,2,0:T(8,128)(2,1)} %copy.49) | copy-start | bytes 3145732
  77.0 6.0 %collective-permute-start.2 = (bf16[128,512]{1,0:T(8,128)(2,1)S(1)}, bf16[128,512]{1,0:T(8,128)(2,1)S(1)}, u32[]{:S(2)}, u32[]{:S(2)}) collective-permute-start(bf16[128,512]{1,0:T(8,128)(2,1)S(1)} %convolution_convert_fusion), channel_id=1, source_target_pairs={{0,2},{1,3},{2,4},{3,5},{4,6},{5,7},{8,10},{9,11},{10,12},{11,13},... | collective-permute-start | bytes 393224 | tf_op jit(solution)/shard_map/ppermute | solution.py:30
  79.2 4.4 %collective-permute-start.3 = (bf16[128,512]{1,0:T(8,128)(2,1)S(1)}, bf16[128,512]{1,0:T(8,128)(2,1)S(1)}, u32[]{:S(2)}, u32[]{:S(2)}) collective-permute-start(bf16[128,512]{1,0:T(8,128)(2,1)S(1)} %convolution_convert_fusion), channel_id=1, source_target_pairs={{0,1},{1,2},{2,3},{3,4},{4,5},{5,6},{6,7},{8,9},{9,10},{10,11},{11... | collective-permute-start | bytes 393224 | tf_op jit(solution)/shard_map/ppermute | solution.py:30
  88.3 3.6 %copy-start.4 = (bf16[640,1,128]{2,1,0:T(2,128)(2,1)S(1)}, bf16[640,1,128]{2,1,0:T(2,128)(2,1)}, u32[]{:S(2)}) copy-start(bf16[640,1,128]{2,1,0:T(2,128)(2,1)} %get-tuple-element.89) | copy-start | bytes 491524
  99.8 2.5 %copy-start.5 = (f32[128,8,640]{0,2,1:T(8,128)S(1)}, f32[128,8,640]{0,2,1:T(8,128)}, u32[]{:S(2)}) copy-start(f32[128,8,640]{0,2,1:T(8,128)} %get-tuple-element.98) | copy-start | bytes 7864324
  102.3 1.7 copy-start.6
  104.0 1.7 copy-start.7
  106.3 6.3 %copy-start = (bf16[1,128,4096]{2,1,0:T(8,128)(2,1)S(1)}, bf16[1,128,4096]{2,1,0:T(8,128)(2,1)}, u32[]{:S(2)}) copy-start(bf16[1,128,4096]{2,1,0:T(8,128)(2,1)} %param.7) | copy-start | bytes 3145732
  107.4 17.0 %collective-permute-start.4 = (f32[128,512]{0,1:T(8,128)}, f32[128,512]{0,1:T(8,128)S(1)}, u32[]{:S(2)}, u32[]{:S(2)}) collective-permute-start(f32[128,512]{0,1:T(8,128)} %get-tuple-element.83), channel_id=1, source_target_pairs={{1,0},{2,1},{3,2},{4,3},{5,4},{6,5},{7,6},{9,8},{10,9},{11,10},{12... | collective-permute-start | bytes 786440 | tf_op jit(solution)/shard_map/ppermute | solution.py:30
  108.7 15.7 %collective-permute-start.5 = (f32[128,512]{0,1:T(8,128)}, f32[128,512]{0,1:T(8,128)S(1)}, u32[]{:S(2)}, u32[]{:S(2)}) collective-permute-start(f32[128,512]{0,1:T(8,128)} %get-tuple-element.86), channel_id=1, source_target_pairs={{2,0},{3,1},{4,2},{5,3},{6,4},{7,5},{10,8},{11,9},{12,10},{13,11},... | collective-permute-start | bytes 786440 | tf_op jit(solution)/shard_map/ppermute | solution.py:30
  110.0 15.8 %collective-permute-start.6 = (f32[128,512]{0,1:T(8,128)}, f32[128,512]{0,1:T(8,128)S(1)}, u32[]{:S(2)}, u32[]{:S(2)}) collective-permute-start(f32[128,512]{0,1:T(8,128)} %get-tuple-element.85), channel_id=1, source_target_pairs={{3,0},{4,1},{5,2},{6,3},{7,4},{11,8},{12,9},{13,10},{14,11},{15,12... | collective-permute-start | bytes 786440 | tf_op jit(solution)/shard_map/ppermute | solution.py:30
  111.3 46.2 %collective-permute-start.7 = (f32[128,512]{0,1:T(8,128)}, f32[128,512]{0,1:T(8,128)S(1)}, u32[]{:S(2)}, u32[]{:S(2)}) collective-permute-start(f32[128,512]{0,1:T(8,128)} %get-tuple-element.84), channel_id=1, source_target_pairs={{4,0},{5,1},{6,2},{7,3},{12,8},{13,9},{14,10},{15,11},{20,16},{21,... | collective-permute-start | bytes 786440 | tf_op jit(solution)/shard_map/ppermute | solution.py:30
  113.9 56.6 %all-to-all-start = ((bf16[128,8,512]{0,2,1:T(8,128)(2,1)}), bf16[128,8,512]{0,2,1:T(8,128)(2,1)S(1)}, u32[]{:S(2)}, u32[]{:S(2)}) async-start(bf16[128,8,512]{0,2,1:T(8,128)(2,1)} %bitcast.35), calls=%async_computation | async-start | bytes 2097152 | tf_op jit(solution)/shard_map/all_to_all | solution.py:104
  124.4 55.3 %all-gather.7.cloned.1.call-start = ((), (), s32[]{:S(2)}) async-start(), calls=%async_computation.3 | async-start | bytes 1179648 | tf_op jit(solution)/shard_map/all_gather | solution.py:108
  158.2 52.4 %reduce-scatter.2.cloned.1.call-start = ((), (), s32[]{:S(2)}) async-start(), calls=%async_computation.4 | async-start | bytes 1310720 | tf_op jit(solution)/shard_map/reduce_scatter | solution.py:111
Sparse Core Ops, SparseCore 0:
  9.2 55.4 all-gather.4
  158.3 21.3 all-gather.6
  182.7 27.8 reduce-scatter.1
where the time goes:
time: 220 us; the launch traced here: 219 us
  waiting for transfers between devices  121 us (55%)
  starting transfers between devices  26.6 us (12%)
  local copies, waits for them, and re-layouts  21.8 us (10%)
  matrix products  21.6 us (10%)
  between operations  13.9 us (6%)
  blocking collectives  10.6 us (5%)
  other arithmetic  3.09 us (1%)
    all_gather x1, waiting for transfers between devices, on_device(): full_weight = lax.all_gather(key_weight, 'section', axis=0, tiled=True)  38 us
    ppermute x8, waiting for transfers between devices, shifted(): return lax.ppermute(x, axis, pairs)  33.6 us
    reduce_scatter x1, waiting for transfers between devices, on_device(): lax.psum_scatter(grad_block, 'section', scatter_dimension=1, tiled=True)  28 us
    ppermute x8, starting transfers between devices, shifted(): return lax.ppermute(x, axis, pairs)  16.1 us
    unnamed x30, local copies, waits for them, and re-layouts  13.1 us
    all_to_all x1, waiting for transfers between devices, on_device(): lax.all_to_all(tokens, 'seq', split_axis=1, concat_axis=0, tiled=True)  12.3 us
    sub x4, matrix products, on_device(): weights_exp = jnp.where(mask_full, jnp.exp(masked - row_top), 0.0)  11.4 us
    all_gather x1, blocking collectives, prefix_2(): gathered = jax.tree.map(lambda a: lax.all_gather(a, axis), part)  10.6 us
  transfers between devices with their start and end apart: 12, of which 7 were waited for; matrix products, arithmetic and copies ran while one was open for 7% of the time, Pallas kernels for 0%

commit v1 on v0

v1 whole, which is shorter than its diff:
```python
import functools
import math

import jax
import jax.numpy as jnp
from jax import lax
from jax.experimental import pallas as pl
from jax.experimental.pallas import tpu as pltpu
from jax.sharding import PartitionSpec as P

HQ = 32
KVH = 4
HD = 128
MOST = 512
GROUP = HQ // KVH
PAIR = 2
MESH = pl.DeviceIdType.MESH
F32 = jnp.float32
BF16 = jnp.bfloat16


def flip(index, bits):
    bit = 1
    while bit <= bits:
        if bits & bit:
            index = index + bit * (1 - 2 * lax.rem(lax.div(index, bit), 2))
        bit *= 2
    return index


def kernel(
    n_sec, n_seq, reach,
    tok_hbm, qry_hbm, grd_hbm, doc_ref, kw_hbm,
    out_ref,
    tok, qry, grd, w_buf, f_buf, f_t, keys, docs, bias, ret_send, ret_recv, own, vg,
    rs_send, rs_recv,
    local_sem, w_ssem, w_rsem, x_ssem, x_rsem, f_ssem, f_rsem, d_ssem, d_rsem,
    k_ssem, k_rsem, r_ssem, r_rsem, v_ssem, v_rsem, s_ssem, s_rsem,
):
    sec, seq = lax.axis_index("section"), lax.axis_index("seq")
    core = lax.rem(seq, 2)
    n_tok = tok.shape[0]
    half = w_buf.shape[2]
    shard = 2 * half
    f_cols = f_buf.shape[2]
    per_head = n_sec // KVH
    cs = rs_send.shape[2]

    def remote(src, dst, ssem, rsem, to_sec, to_seq):
        return pltpu.make_async_remote_copy(
            src_ref=src, dst_ref=dst, send_sem=ssem, recv_sem=rsem,
            device_id=(to_sec, to_seq), device_id_type=MESH,
        )

    loc_w = pltpu.make_async_copy(kw_hbm, w_buf.at[0], local_sem.at[0])
    loc_t = pltpu.make_async_copy(tok_hbm, tok, local_sem.at[1])
    loc_q = pltpu.make_async_copy(qry_hbm, qry, local_sem.at[2])
    loc_g = pltpu.make_async_copy(grd_hbm, grd, local_sem.at[3])

    barrier = pltpu.get_barrier_semaphore()
    for d in range(1, n_sec):
        pl.semaphore_signal(barrier, inc=1, device_id=(flip(sec, d), seq), device_id_type=MESH)
    for d in range(1, n_seq):
        pl.semaphore_signal(barrier, inc=1, device_id=(sec, flip(seq, d)), device_id_type=MESH)
    loc_w.start()
    loc_t.start()
    loc_q.start()
    loc_g.start()
    pl.semaphore_wait(barrier, n_sec + n_seq - 2)

    sends = []

    def launch(copy):
        copy.start()
        sends.append((None, copy))

    w_in = [None] + [
        remote(kw_hbm.at[core], w_buf.at[d, core], w_ssem.at[d - 1], w_rsem.at[d - 1], flip(sec, d), seq)
        for d in range(1, n_sec)
    ]
    for d in range(1, n_sec):
        launch(w_in[d])

    def hop(h, src, dst, ssem, rsem, by):
        copy = remote(src, dst, ssem, rsem, sec, seq + by)
        return copy

    docs[0] = doc_ref[...]
    d_out = []
    for h in range(1, reach + 1):
        copy = remote(doc_ref, docs.at[h], d_ssem.at[h - 1], d_rsem.at[h - 1], sec, seq + h)
        d_out.append(copy)
        has_later = seq + h < n_seq
        pl.when(has_later)(copy.start)
        sends.append((has_later, copy))

    f_in = [None]
    for d in range(1, n_seq):
        peer = flip(seq, d)
        cols = pl.ds(pl.multiple_of(peer * f_cols, f_cols), f_cols)
        copy = remote(tok_hbm.at[:, cols], f_buf.at[d], f_ssem.at[d - 1], f_rsem.at[d - 1], sec, peer)
        launch(copy)
        f_in.append(copy)

    for h in range(1, reach + 1):
        @pl.when(seq < h)
        def _(h=h):
            docs[h] = jnp.full(docs.shape[1:], -1, jnp.int32)
            keys[h] = jnp.zeros(keys.shape[1:], BF16)

        @pl.when(seq + h >= n_seq)
        def _(h=h):
            for k in range(KVH):
                ret_recv[k, h - 1] = jnp.zeros(ret_recv.shape[2:], BF16)

    loc_t.wait()
    loc_w.wait()

    def project(d, which):
        row = pl.multiple_of(flip(sec, d) * shard + which * half, half)
        return jnp.dot(tok[:, pl.ds(row, half)], w_buf[d, which], preferred_element_type=F32)

    total = project(0, 0) + project(0, 1)

    own_row = docs[0]
    query_doc = own_row.astype(F32)
    key_at = lax.broadcasted_iota(jnp.int32, (n_tok, n_tok), 0)
    query_at = lax.broadcasted_iota(jnp.int32, (n_tok, n_tok), 1)
    for h in range(reach + 1):
        if h:
            pl.when(seq >= h)(d_out[h - 1].wait_recv)
        key_doc = jnp.broadcast_to(docs[h].astype(F32), (n_tok, n_tok)).T
        seen = key_doc == jnp.broadcast_to(query_doc, (n_tok, n_tok))
        if h == 0:
            seen = seen & (key_at <= query_at)
        bias[pl.ds(h * n_tok, n_tok), :] = jnp.where(seen, 0.0, -1e30)

    x_in = [None]
    for d in range(1, n_sec):
        w_in[d].wait_recv()
        copy = remote(
            w_buf.at[d, core], w_buf.at[d, core], x_ssem.at[d - 1], x_rsem.at[d - 1], sec, flip(seq, 1)
        )
        launch(copy)
        x_in.append(remote(
            w_buf.at[d, 1 - core], w_buf.at[d, 1 - core], x_ssem.at[d - 1], x_rsem.at[d - 1],
            sec, flip(seq, 1),
        ))
        total = total + project(d, core)
    for d in range(1, n_sec):
        x_in[d].wait_recv()
        total = total + project(d, 1 - core)
    keys[0] = total.astype(BF16)

    k_in = []
    for h in range(1, reach + 1):
        copy = remote(keys.at[0], keys.at[h], k_ssem.at[h - 1], k_rsem.at[h - 1], sec, seq + h)
        has_later = seq + h < n_seq
        pl.when(has_later)(copy.start)
        sends.append((has_later, copy))
        k_in.append(copy)

    own_cols = pl.ds(pl.multiple_of(seq * f_cols, f_cols), f_cols)
    f_t[:, 0:n_tok] = tok[:, own_cols].T
    for d in range(1, n_seq):
        f_in[d].wait_recv()
        f_t[:, d * n_tok : (d + 1) * n_tok] = f_buf[d].T

    loc_q.wait()
    loc_g.wait()
    for h in range(1, reach + 1):
        pl.when(seq >= h)(k_in[h - 1].wait_recv)

    scale = math.log2(math.e) / math.sqrt(HD)
    window = (reach + 1) * n_tok

    def head_of(k):
        return lax.rem(lax.div(sec, per_head) + 1 + k, KVH)

    r_in = {}

    def attend(k):
        head = head_of(k)
        key_head = keys[:, :, pl.ds(pl.multiple_of(head * HD, HD), HD)].reshape(window, HD)
        mask = jnp.concatenate([bias[...]] * PAIR, axis=1)
        acc = jnp.zeros((window, HD), F32)
        for r in range(0, GROUP, PAIR):
            def rows(ref):
                base = head * (GROUP * HD)
                parts = [
                    ref[:, pl.ds(pl.multiple_of(base + (r + i) * HD, HD), HD)] for i in range(PAIR)
                ]
                return jnp.concatenate(parts, axis=0)

            scores = lax.dot_general(
                key_head, rows(qry), (((1,), (1,)), ((), ())), preferred_element_type=F32
            ) * scale + mask
            top = jnp.max(scores, axis=0, keepdims=True)
            e = jnp.exp2(scores - top)
            p = e * (1.0 / jnp.sum(e, axis=0, keepdims=True))
            acc = acc + jnp.dot(p.astype(BF16), rows(grd), preferred_element_type=F32)
        own[k] = acc[0:n_tok]
        for h in range(1, reach + 1):
            ret_send[k, h - 1] = acc[h * n_tok : (h + 1) * n_tok].astype(BF16)
            copy = remote(
                ret_send.at[k, h - 1], ret_recv.at[k, h - 1],
                r_ssem.at[k, h - 1], r_rsem.at[k, h - 1], sec, seq - h,
            )
            pl.when(seq >= h)(copy.start)
            sends.append((seq >= h, copy))
            r_in[k, h] = copy

    v_in = {}

    def combine(k):
        value = own[k]
        for h in range(1, reach + 1):
            pl.when(seq + h < n_seq)(r_in[k, h].wait_recv)
            value = value + ret_recv[k, h - 1].astype(F32)
        vg[k, 0] = value.astype(BF16)
        for d in range(1, n_seq):
            copy = remote(
                vg.at[k, 0], vg.at[k, d], v_ssem.at[k, d - 1], v_rsem.at[k, d - 1], sec, flip(seq, d)
            )
            launch(copy)
            v_in[k, d] = copy

    def finish(k):
        for d in range(1, n_seq):
            v_in[k, d].wait_recv()
        result = jnp.dot(
            f_t[...], vg[k].reshape(n_seq * n_tok, HD), preferred_element_type=F32
        )
        head = head_of(k)
        for i in range(per_head):
            piece = result[:, i * cs : (i + 1) * cs]
            slot = k * per_head + i
            to = head * per_head + i

            def give(slot=slot, to=to, piece=piece):
                rs_send[slot] = piece.astype(BF16)
                remote(
                    rs_send.at[slot], rs_recv.at[sec], s_ssem.at[slot], s_rsem.at[sec], to, seq
                ).start()

            copy = remote(
                rs_send.at[slot], rs_recv.at[sec], s_ssem.at[slot], s_rsem.at[sec], to, seq
            )
            if k < KVH - 1:
                give()
                sends.append((None, copy))
            else:
                if per_head > 1:
                    pl.when(to != sec)(give)
                    sends.append((to != sec, copy))

                @pl.when(to == sec)
                def _(piece=piece):
                    out_ref[...] = piece

    for step in range(KVH + 2):
        if step < KVH:
            attend(step)
        if 0 <= step - 1 < KVH:
            combine(step - 1)
        if 0 <= step - 2 < KVH:
            finish(step - 2)

    final = out_ref[...]
    for d in range(1, n_sec):
        src = flip(sec, d)
        remote(rs_recv.at[src], rs_recv.at[src], s_ssem.at[0], s_rsem.at[src], src, seq).wait_recv()
        final = final + rs_recv[src].astype(F32)
    out_ref[...] = final

    for condition, copy in sends:
        if condition is None:
            copy.wait_send()
        else:
            pl.when(condition)(copy.wait_send)


def on_device(n_sec, n_seq, features, queries, out_grad, doc_ids, key_weight):
    tokens = features[0]
    n_tok, width = tokens.shape
    rows, kv_width = key_weight.shape
    reach = min(n_seq - 1, -(-(MOST - 1) // n_tok))
    half = rows // 2
    f_cols = width // n_seq
    cs = kv_width // n_sec
    dma = lambda *shape: pltpu.SemaphoreType.DMA(shape)
    any_spec = pl.BlockSpec(memory_space=pl.ANY)
    vmem_spec = pl.BlockSpec(memory_space=pltpu.VMEM)
    return pl.pallas_call(
        functools.partial(kernel, n_sec, n_seq, reach),
        out_shape=jax.ShapeDtypeStruct((f_cols, cs), F32),
        in_specs=[any_spec, any_spec, any_spec, vmem_spec, any_spec],
        out_specs=vmem_spec,
        scratch_shapes=[
            pltpu.VMEM((n_tok, width), BF16),
            pltpu.VMEM((n_tok, HQ * HD), BF16),
            pltpu.VMEM((n_tok, HQ * HD), BF16),
            pltpu.VMEM((n_sec, 2, half, kv_width), BF16),
            pltpu.VMEM((n_seq, n_tok, f_cols), BF16),
            pltpu.VMEM((f_cols, n_seq * n_tok), BF16),
            pltpu.VMEM((reach + 1, n_tok, kv_width), BF16),
            pltpu.VMEM((reach + 1, 1, n_tok), jnp.int32),
            pltpu.VMEM(((reach + 1) * n_tok, n_tok), F32),
            pltpu.VMEM((KVH, reach, n_tok, HD), BF16),
            pltpu.VMEM((KVH, reach, n_tok, HD), BF16),
            pltpu.VMEM((KVH, n_tok, HD), F32),
            pltpu.VMEM((KVH, n_seq, n_tok, HD), BF16),
            pltpu.VMEM((n_sec, f_cols, cs), BF16),
            pltpu.VMEM((n_sec, f_cols, cs), BF16),
            dma(4),
            dma(n_sec - 1), dma(n_sec - 1),
            dma(n_sec - 1), dma(n_sec - 1),
            dma(n_seq - 1), dma(n_seq - 1),
            dma(reach), dma(reach),
            dma(reach), dma(reach),
            dma(KVH, reach), dma(KVH, reach),
            dma(KVH, n_seq - 1), dma(KVH, n_seq - 1),
            dma(n_sec), dma(n_sec),
        ],
        compiler_params=pltpu.CompilerParams(
            collective_id=0, has_side_effects=True, vmem_limit_bytes=48 * 1024 * 1024
        ),
    )(tokens, queries[0], out_grad[0], doc_ids, key_weight.reshape(2, half, kv_width))


def solution(mesh):
    n_sec, n_seq = mesh.shape["section"], mesh.shape["seq"]
    return jax.shard_map(
        functools.partial(on_device, n_sec, n_seq),
        mesh=mesh,
        in_specs=(
            P("section", "seq", None),
            P("section", "seq", None),
            P("section", "seq", None),
            P("section", "seq"),
            P("section", None),
        ),
        out_specs=P("seq", "section"),
        check_vma=False,
    )
```

time: 220 us -> 95.9 us (0.44)
  waiting for transfers between devices: 121 us -> 0 us
  Pallas kernels: 0 us -> 89.4 us
  starting transfers between devices: 26.6 us -> 0 us
  matrix products: 21.6 us -> 0 us
  local copies, waits for them, and re-layouts: 21.8 us -> 6.26 us
  between operations: 13.9 us -> 0.01 us
  blocking collectives: 10.6 us -> 0 us
  other arithmetic: 3.09 us -> 0 us
    pallas_call x0 -> x1, Pallas kernels: none -> 89.4 us  [on_device(): pl.pallas_call(functools.partial(kernel, n_sec, n_seq, reach), out_shape=...]
    all_gather x2 -> x0, waiting for transfers between devices: 46.6 us -> none  [the longest x1 38 us: on_device(): full_weight = lax.all_gather(key_weight, 'section', axis=0, tiled=True)]
    ppermute x8 -> x0, waiting for transfers between devices: 33.6 us -> none  [shifted(): return lax.ppermute(x, axis, pairs)]
    reduce_scatter x1 -> x0, waiting for transfers between devices: 28 us -> none  [on_device(): lax.psum_scatter(grad_block, 'section', scatter_dimension=1, tiled=True)]
    ppermute x8 -> x0, starting transfers between devices: 16.1 us -> none  [shifted(): return lax.ppermute(x, axis, pairs)]
    all_to_all x1 -> x0, waiting for transfers between devices: 12.3 us -> none  [on_device(): lax.all_to_all(tokens, 'seq', split_axis=1, concat_axis=0, tiled=True)]
    sub x4 -> x0, matrix products: 11.4 us -> none  [on_device(): weights_exp = jnp.where(mask_full, jnp.exp(masked - row_top), 0.0)]
    all_gather x1 -> x0, blocking collectives: 10.6 us -> none  [prefix_2(): gathered = jax.tree.map(lambda a: lax.all_gather(a, axis), part)]
  transfers between devices with their start and end apart: 12 -> 0, of which waited for: 7 -> 0; matrix products, arithmetic and copies ran while one was open for 7% -> 0% of each run, Pallas kernels for 0% -> 0%
where the time goes in v1:
time: 95.9 us; the launch traced here: 95.7 us
  Pallas kernels  89.4 us (93%)
  local copies, waits for them, and re-layouts  6.26 us (7%)
    pallas_call x1, Pallas kernels, on_device(): pl.pallas_call(functools.partial(kernel, n_sec, n_seq, reach), out_shape=...  89.4 us
    unnamed x11, local copies, waits for them, and re-layouts  6.26 us

profile of v1, /device:TPU:0, one launch (start us, length us, event | category | flops | bytes accessed | tf_op | source)
XLA Modules:
  0.0 95.7 jit_solution(11628817909736424591)
XLA Ops:
  0.0 0.0 copy-start.4
  0.0 0.7 copy-done.4
  0.7 0.0 copy-start
  0.7 1.2 %copy-done = bf16[1,128,4096]{2,1,0:T(8,128)(2,1)S(1)} copy-done((bf16[1,128,4096]{2,1,0:T(8,128)(2,1)S(1)}, bf16[1,128,4096]{2,1,0:T(8,128)(2,1)}, u32[]{:S(2)}) %copy-start) | copy-done | bytes 1048600
  1.9 0.0 copy-start.1
  1.9 1.2 %copy-done.1 = bf16[1,128,4096]{2,1,0:T(8,128)(2,1)S(1)} copy-done((bf16[1,128,4096]{2,1,0:T(8,128)(2,1)S(1)}, bf16[1,128,4096]{2,1,0:T(8,128)(2,1)}, u32[]{:S(2)}) %copy-start.1) | copy-done | bytes 1048600
  3.1 0.0 copy-start.2
  3.1 1.2 %copy-done.2 = bf16[1,128,4096]{2,1,0:T(8,128)(2,1)S(1)} copy-done((bf16[1,128,4096]{2,1,0:T(8,128)(2,1)S(1)}, bf16[1,128,4096]{2,1,0:T(8,128)(2,1)}, u32[]{:S(2)}) %copy-start.2) | copy-done | bytes 1048600
  4.3 0.0 copy-start.3
  4.3 1.2 %copy-done.3 = bf16[1024,512]{1,0:T(8,128)(2,1)S(1)} copy-done((bf16[1024,512]{1,0:T(8,128)(2,1)S(1)}, bf16[1024,512]{1,0:T(8,128)(2,1)}, u32[]{:S(2)}) %copy-start.3) | copy-done | bytes 1048600
  5.6 89.4 %shard_map.55 = f32[512,128]{1,0:T(8,128)S(1)} custom-call(bf16[128,4096]{1,0:T(8,128)(2,1)S(1)} %bitcast.4, bf16[128,4096]{1,0:T(8,128)(2,1)S(1)} %bitcast.5, bf16[128,4096]{1,0:T(8,128)(2,1)S(1)} %bitcast.6, s32[1,128]{1,0:T(1,128)S(1)} %copy-done.4, bf16[2,512,512]{2,1,0:T(8,128)(2,1)S(1)} %bitcast.7), custom_call_target="tpu_custom_call" | custom-call | tf_op jit(solution)/shard_map/pallas_call | solution.py:294
  95.0 0.7 copy.7
Async XLA Ops:
  0.0 0.7 copy-start.4
  0.7 1.2 %copy-start = (bf16[1,128,4096]{2,1,0:T(8,128)(2,1)S(1)}, bf16[1,128,4096]{2,1,0:T(8,128)(2,1)}, u32[]{:S(2)}) copy-start(bf16[1,128,4096]{2,1,0:T(8,128)(2,1)} %param.5) | copy-start | bytes 3145732
  1.9 1.2 %copy-start.1 = (bf16[1,128,4096]{2,1,0:T(8,128)(2,1)S(1)}, bf16[1,128,4096]{2,1,0:T(8,128)(2,1)}, u32[]{:S(2)}) copy-start(bf16[1,128,4096]{2,1,0:T(8,128)(2,1)} %param.6) | copy-start | bytes 3145732
  3.1 1.2 %copy-start.2 = (bf16[1,128,4096]{2,1,0:T(8,128)(2,1)S(1)}, bf16[1,128,4096]{2,1,0:T(8,128)(2,1)}, u32[]{:S(2)}) copy-start(bf16[1,128,4096]{2,1,0:T(8,128)(2,1)} %param.7) | copy-start | bytes 3145732
  4.3 1.2 %copy-start.3 = (bf16[1024,512]{1,0:T(8,128)(2,1)S(1)}, bf16[1024,512]{1,0:T(8,128)(2,1)}, u32[]{:S(2)}) copy-start(bf16[1024,512]{1,0:T(8,128)(2,1)} %param.9) | copy-start | bytes 3145732

commit v2 on v1

--- a/solution.py
+++ b/solution.py
@@ -33,16 +33,18 @@
     tok_hbm, qry_hbm, grd_hbm, doc_ref, kw_hbm,
     out_ref,
     tok, qry, grd, w_buf, f_buf, f_t, keys, docs, bias, ret_send, ret_recv, own, vg,
-    rs_send, rs_recv,
+    rs_send, rs_recv, ex_send, ex_recv, total_ref,
     local_sem, w_ssem, w_rsem, x_ssem, x_rsem, f_ssem, f_rsem, d_ssem, d_rsem,
-    k_ssem, k_rsem, r_ssem, r_rsem, v_ssem, v_rsem, s_ssem, s_rsem,
+    k_ssem, k_rsem, r_ssem, r_rsem, v_ssem, v_rsem, s_ssem, s_rsem, e_ssem, e_rsem,
 ):
     sec, seq = lax.axis_index("section"), lax.axis_index("seq")
     core = lax.rem(seq, 2)
     n_tok = tok.shape[0]
     half = w_buf.shape[2]
     shard = 2 * half
-    f_cols = f_buf.shape[2]
+    f_cols = f_buf.shape[3]
+    group = n_seq // 2
+    other = flip(seq, group)
     per_head = n_sec // KVH
     cs = rs_send.shape[2]
 
@@ -81,10 +83,6 @@
     for d in range(1, n_sec):
         launch(w_in[d])
 
-    def hop(h, src, dst, ssem, rsem, by):
-        copy = remote(src, dst, ssem, rsem, sec, seq + by)
-        return copy
-
     docs[0] = doc_ref[...]
     d_out = []
     for h in range(1, reach + 1):
@@ -94,13 +92,19 @@
         pl.when(has_later)(copy.start)
         sends.append((has_later, copy))
 
-    f_in = [None]
-    for d in range(1, n_seq):
+    def columns_of(place):
+        return pl.ds(pl.multiple_of(place * f_cols, f_cols), f_cols)
+
+    f_in = {}
+    for d in range(1, group):
         peer = flip(seq, d)
-        cols = pl.ds(pl.multiple_of(peer * f_cols, f_cols), f_cols)
-        copy = remote(tok_hbm.at[:, cols], f_buf.at[d], f_ssem.at[d - 1], f_rsem.at[d - 1], sec, peer)
-        launch(copy)
-        f_in.append(copy)
+        for c in range(2):
+            copy = remote(
+                tok_hbm.at[:, columns_of(flip(peer, c * group))], f_buf.at[d, c],
+                f_ssem.at[d - 1, c], f_rsem.at[d - 1, c], sec, peer,
+            )
+            launch(copy)
+            f_in[d, c] = copy
 
     for h in range(1, reach + 1):
         @pl.when(seq < h)
@@ -160,11 +164,12 @@
         sends.append((has_later, copy))
         k_in.append(copy)
 
-    own_cols = pl.ds(pl.multiple_of(seq * f_cols, f_cols), f_cols)
-    f_t[:, 0:n_tok] = tok[:, own_cols].T
-    for d in range(1, n_seq):
-        f_in[d].wait_recv()
-        f_t[:, d * n_tok : (d + 1) * n_tok] = f_buf[d].T
+    for c in range(2):
+        rows_c = pl.ds(c * f_cols, f_cols)
+        f_t[rows_c, 0:n_tok] = tok[:, columns_of(flip(seq, c * group))].T
+        for d in range(1, group):
+            f_in[d, c].wait_recv()
+            f_t[rows_c, d * n_tok : (d + 1) * n_tok] = f_buf[d, c].T
 
     loc_q.wait()
     loc_g.wait()
@@ -218,7 +223,7 @@
             pl.when(seq + h < n_seq)(r_in[k, h].wait_recv)
             value = value + ret_recv[k, h - 1].astype(F32)
         vg[k, 0] = value.astype(BF16)
-        for d in range(1, n_seq):
+        for d in range(1, group):
             copy = remote(
                 vg.at[k, 0], vg.at[k, d], v_ssem.at[k, d - 1], v_rsem.at[k, d - 1], sec, flip(seq, d)
             )
@@ -226,10 +231,10 @@
             v_in[k, d] = copy
 
     def finish(k):
-        for d in range(1, n_seq):
+        for d in range(1, group):
             v_in[k, d].wait_recv()
         result = jnp.dot(
-            f_t[...], vg[k].reshape(n_seq * n_tok, HD), preferred_element_type=F32
+            f_t[...], vg[k].reshape(group * n_tok, HD), preferred_element_type=F32
         )
         head = head_of(k)
         for i in range(per_head):
@@ -256,7 +261,7 @@
 
                 @pl.when(to == sec)
                 def _(piece=piece):
-                    out_ref[...] = piece
+                    total_ref[...] = piece
 
     for step in range(KVH + 2):
         if step < KVH:
@@ -266,12 +271,22 @@
         if 0 <= step - 2 < KVH:
             finish(step - 2)
 
-    final = out_ref[...]
-    for d in range(1, n_sec):
-        src = flip(sec, d)
+    sources = [flip(sec, d) for d in range(1, n_sec)]
+    for src in sources:
         remote(rs_recv.at[src], rs_recv.at[src], s_ssem.at[0], s_rsem.at[src], src, seq).wait_recv()
-        final = final + rs_recv[src].astype(F32)
-    out_ref[...] = final
+    theirs = pl.ds(f_cols, f_cols)
+    away = total_ref[theirs, :]
+    for src in sources:
+        away = away + rs_recv[src, theirs, :].astype(F32)
+    ex_send[...] = away.astype(BF16)
+    swap = remote(ex_send, ex_recv, e_ssem.at[0], e_rsem.at[0], sec, other)
+    launch(swap)
+    mine = pl.ds(0, f_cols)
+    final = total_ref[mine, :]
+    for src in sources:
+        final = final + rs_recv[src, mine, :].astype(F32)
+    swap.wait_recv()
+    out_ref[...] = final + ex_recv[...].astype(F32)
 
     for condition, copy in sends:
         if condition is None:
@@ -287,9 +302,10 @@
     reach = min(n_seq - 1, -(-(MOST - 1) // n_tok))
     half = rows // 2
     f_cols = width // n_seq
+    group = n_seq // 2
     cs = kv_width // n_sec
     dma = lambda *shape: pltpu.SemaphoreType.DMA(shape)
-    any_spec = pl.BlockSpec(memory_space=pl.ANY)
+    any_spec = pl.BlockSpec(memory_space=pltpu.HBM)
     vmem_spec = pl.BlockSpec(memory_space=pltpu.VMEM)
     return pl.pallas_call(
         functools.partial(kernel, n_sec, n_seq, reach),
@@ -301,29 +317,33 @@
             pltpu.VMEM((n_tok, HQ * HD), BF16),
             pltpu.VMEM((n_tok, HQ * HD), BF16),
             pltpu.VMEM((n_sec, 2, half, kv_width), BF16),
-            pltpu.VMEM((n_seq, n_tok, f_cols), BF16),
-            pltpu.VMEM((f_cols, n_seq * n_tok), BF16),
+            pltpu.VMEM((group, 2, n_tok, f_cols), BF16),
+            pltpu.VMEM((2 * f_cols, group * n_tok), BF16),
             pltpu.VMEM((reach + 1, n_tok, kv_width), BF16),
             pltpu.VMEM((reach + 1, 1, n_tok), jnp.int32),
             pltpu.VMEM(((reach + 1) * n_tok, n_tok), F32),
             pltpu.VMEM((KVH, reach, n_tok, HD), BF16),
             pltpu.VMEM((KVH, reach, n_tok, HD), BF16),
             pltpu.VMEM((KVH, n_tok, HD), F32),
-            pltpu.VMEM((KVH, n_seq, n_tok, HD), BF16),
-            pltpu.VMEM((n_sec, f_cols, cs), BF16),
-            pltpu.VMEM((n_sec, f_cols, cs), BF16),
+            pltpu.VMEM((KVH, group, n_tok, HD), BF16),
+            pltpu.VMEM((n_sec, 2 * f_cols, cs), BF16),
+            pltpu.VMEM((n_sec, 2 * f_cols, cs), BF16),
+            pltpu.VMEM((f_cols, cs), BF16),
+            pltpu.VMEM((f_cols, cs), BF16),
+            pltpu.VMEM((2 * f_cols, cs), F32),
             dma(4),
             dma(n_sec - 1), dma(n_sec - 1),
             dma(n_sec - 1), dma(n_sec - 1),
-            dma(n_seq - 1), dma(n_seq - 1),
+            dma(group - 1, 2), dma(group - 1, 2),
             dma(reach), dma(reach),
             dma(reach), dma(reach),
             dma(KVH, reach), dma(KVH, reach),
-            dma(KVH, n_seq - 1), dma(KVH, n_seq - 1),
+            dma(KVH, group - 1), dma(KVH, group - 1),
             dma(n_sec), dma(n_sec),
+            dma(1), dma(1),
         ],
         compiler_params=pltpu.CompilerParams(
-            collective_id=0, has_side_effects=True, vmem_limit_bytes=48 * 1024 * 1024
+            collective_id=0, has_side_effects=True, vmem_limit_bytes=60 * 1024 * 1024
         ),
     )(tokens, queries[0], out_grad[0], doc_ids, key_weight.reshape(2, half, kv_width))
 

time: 95.9 us -> 83.9 us (0.87)
  Pallas kernels: 89.4 us -> 82 us
  local copies, waits for them, and re-layouts: 6.26 us -> 1.67 us
    pallas_call x1, Pallas kernels: 89.4 us -> 82 us  [on_device(): pl.pallas_call(functools.partial(kernel, n_sec, n_seq, reach), out_shape=...]
    unnamed x11 -> x1, local copies, waits for them, and re-layouts: 6.26 us -> 1.67 us
where the time goes in v2:
time: 83.9 us; the launch traced here: 83.7 us
  Pallas kernels  82 us (98%)
  local copies, waits for them, and re-layouts  1.67 us (2%)
    pallas_call x1, Pallas kernels, on_device(): pl.pallas_call(functools.partial(kernel, n_sec, n_seq, reach), out_shape=...  82 us

profile of v2, /device:TPU:0, one launch (start us, length us, event | category | flops | bytes accessed | tf_op | source)
XLA Modules:
  0.0 83.7 jit_solution(11372273542365995167)
XLA Ops:
  0.0 82.0 %shard_map.55 = f32[512,128]{1,0:T(8,128)} custom-call(bf16[128,4096]{1,0:T(8,128)(2,1)} %bitcast.4, bf16[128,4096]{1,0:T(8,128)(2,1)} %bitcast.5, bf16[128,4096]{1,0:T(8,128)(2,1)} %bitcast.6, s32[1,128]{1,0:T(1,128)} %doc_ref.1, bf16[2,512,512]{2,1,0:T(8,128)(2,1)} %bitcast.7), custom_call_target="tpu_custom_call" | custom-call | tf_op jit(solution)/shard_map/pallas_call | solution.py:310
  82.0 1.7 %copy.7 = f32[512,128]{1,0:T(8,128)} copy(f32[512,128]{1,0:T(8,128)} %shard_map.55) | data formatting | bytes 524288

commit v3 on v2

--- a/solution.py
+++ b/solution.py
@@ -80,8 +80,17 @@
         remote(kw_hbm.at[core], w_buf.at[d, core], w_ssem.at[d - 1], w_rsem.at[d - 1], flip(sec, d), seq)
         for d in range(1, n_sec)
     ]
-    for d in range(1, n_sec):
+    relayed = n_sec == 4
+    for d in range(1, n_sec - 1 if relayed else n_sec):
         launch(w_in[d])
+    part = half // 2
+    relay = [
+        remote(
+            w_buf.at[d, core, pl.ds(i * part, part)], w_buf.at[3, core, pl.ds(i * part, part)],
+            w_ssem.at[2 + i], w_rsem.at[2 + i], flip(sec, 3 - d), seq,
+        )
+        for i, d in enumerate((1, 2))
+    ] if relayed else []
 
     docs[0] = doc_ref[...]
     d_out = []
@@ -141,7 +150,13 @@
 
     x_in = [None]
     for d in range(1, n_sec):
-        w_in[d].wait_recv()
+        if relayed and d == 3:
+            for copy in relay:
+                copy.wait_recv()
+        else:
+            w_in[d].wait_recv()
+            if relayed:
+                launch(relay[d - 1])
         copy = remote(
             w_buf.at[d, core], w_buf.at[d, core], x_ssem.at[d - 1], x_rsem.at[d - 1], sec, flip(seq, 1)
         )
@@ -332,7 +347,7 @@
             pltpu.VMEM((f_cols, cs), BF16),
             pltpu.VMEM((2 * f_cols, cs), F32),
             dma(4),
-            dma(n_sec - 1), dma(n_sec - 1),
+            dma(n_sec), dma(n_sec),
             dma(n_sec - 1), dma(n_sec - 1),
             dma(group - 1, 2), dma(group - 1, 2),
             dma(reach), dma(reach),

time: 83.9 us -> 78.8 us (0.939)
  Pallas kernels: 82 us -> 77 us
    pallas_call x1, Pallas kernels: 82 us -> 77 us  [on_device(): pl.pallas_call(functools.partial(kernel, n_sec, n_seq, reach), out_shape=...]
where the time goes in v3:
time: 78.8 us; the launch traced here: 78.7 us
  Pallas kernels  77 us (98%)
  local copies, waits for them, and re-layouts  1.67 us (2%)
    pallas_call x1, Pallas kernels, on_device(): pl.pallas_call(functools.partial(kernel, n_sec, n_seq, reach), out_shape=...  77 us
    unnamed x1, local copies, waits for them, and re-layouts  1.67 us

profile of v3, /device:TPU:0, one launch (start us, length us, event | category | flops | bytes accessed | tf_op | source)
XLA Modules:
  0.0 78.7 jit_solution(6231207014121104906)
XLA Ops:
  0.0 77.0 %shard_map.55 = f32[512,128]{1,0:T(8,128)} custom-call(bf16[128,4096]{1,0:T(8,128)(2,1)} %bitcast.4, bf16[128,4096]{1,0:T(8,128)(2,1)} %bitcast.5, bf16[128,4096]{1,0:T(8,128)(2,1)} %bitcast.6, s32[1,128]{1,0:T(1,128)} %doc_ref.1, bf16[2,512,512]{2,1,0:T(8,128)(2,1)} %bitcast.7), custom_call_target="tpu_custom_call" | custom-call | tf_op jit(solution)/shard_map/pallas_call | solution.py:325
  77.0 1.7 %copy.7 = f32[512,128]{1,0:T(8,128)} copy(f32[512,128]{1,0:T(8,128)} %shard_map.55) | data formatting | bytes 524288

commit v4 on v3

--- a/solution.py
+++ b/solution.py
@@ -171,13 +171,24 @@
         total = total + project(d, 1 - core)
     keys[0] = total.astype(BF16)
 
-    k_in = []
-    for h in range(1, reach + 1):
+    k_in = {}
+    for h in range(2, reach + 1, 2):
         copy = remote(keys.at[0], keys.at[h], k_ssem.at[h - 1], k_rsem.at[h - 1], sec, seq + h)
         has_later = seq + h < n_seq
         pl.when(has_later)(copy.start)
         sends.append((has_later, copy))
-        k_in.append(copy)
+        k_in[h] = copy
+
+    def hand_on():
+        for h in range(1, reach + 1, 2):
+            pl.when(seq >= h + 1)(k_in[h + 1].wait_recv)
+            from_slot = h - 1 + 2 * core
+            copy = remote(
+                keys.at[from_slot], keys.at[h], k_ssem.at[h - 1], k_rsem.at[h - 1], sec, flip(seq, 1)
+            )
+            pl.when(seq >= from_slot)(copy.start)
+            sends.append((seq >= from_slot, copy))
+            k_in[h] = copy
 
     for c in range(2):
         rows_c = pl.ds(c * f_cols, f_cols)
@@ -185,11 +196,13 @@
         for d in range(1, group):
             f_in[d, c].wait_recv()
             f_t[rows_c, d * n_tok : (d + 1) * n_tok] = f_buf[d, c].T
+        if c == 0:
+            hand_on()
 
     loc_q.wait()
     loc_g.wait()
-    for h in range(1, reach + 1):
-        pl.when(seq >= h)(k_in[h - 1].wait_recv)
+    for h in range(1, reach + 1, 2):
+        pl.when(seq >= h)(k_in[h].wait_recv)
 
     scale = math.log2(math.e) / math.sqrt(HD)
     window = (reach + 1) * n_tok
@@ -315,6 +328,7 @@
     n_tok, width = tokens.shape
     rows, kv_width = key_weight.shape
     reach = min(n_seq - 1, -(-(MOST - 1) // n_tok))
+    reach += reach % 2
     half = rows // 2
     f_cols = width // n_seq
     group = n_seq // 2

time: 78.8 us -> 75.5 us (0.958)
  Pallas kernels: 77 us -> 73.7 us
    pallas_call x1, Pallas kernels: 77 us -> 73.7 us  [on_device(): pl.pallas_call(functools.partial(kernel, n_sec, n_seq, reach), out_shape=...]
where the time goes in v4:
time: 75.5 us; the launch traced here: 75.3 us
  Pallas kernels  73.7 us (98%)
  local copies, waits for them, and re-layouts  1.67 us (2%)
    pallas_call x1, Pallas kernels, on_device(): pl.pallas_call(functools.partial(kernel, n_sec, n_seq, reach), out_shape=...  73.7 us
    unnamed x1, local copies, waits for them, and re-layouts  1.67 us

profile of v4, /device:TPU:0, one launch (start us, length us, event | category | flops | bytes accessed | tf_op | source)
XLA Modules:
  0.0 75.3 jit_solution(5005984380510989682)
XLA Ops:
  0.0 73.7 %shard_map.55 = f32[512,128]{1,0:T(8,128)} custom-call(bf16[128,4096]{1,0:T(8,128)(2,1)} %bitcast.4, bf16[128,4096]{1,0:T(8,128)(2,1)} %bitcast.5, bf16[128,4096]{1,0:T(8,128)(2,1)} %bitcast.6, s32[1,128]{1,0:T(1,128)} %doc_ref.1, bf16[2,512,512]{2,1,0:T(8,128)(2,1)} %bitcast.7), custom_call_target="tpu_custom_call" | custom-call | tf_op jit(solution)/shard_map/pallas_call | solution.py:339
  73.7 1.7 %copy.7 = f32[512,128]{1,0:T(8,128)} copy(f32[512,128]{1,0:T(8,128)} %shard_map.55) | data formatting | bytes 524288
